TPU v7x, 128 devices: a whole 4x4x4 slice. The times are simulated.
128 devices in a mesh: row: 16 (over x, z), col: 8 (over y, core).
Axes of the slice: x: 4, y: 4, z: 4, core: 2. Of those that a mesh axis runs over, the one named last changes fastest.
Arguments:
- tmatrix: bfloat16 [10656, 10656], P('row', 'col'), may hold values from -0.0625 to 0.0625
- panel: bfloat16 [10656, 2048], P('col', 'row'), may hold values from -6 to 6
- contrast: float32 [3, 144, 288], replicated, may hold values from -1.5 to 1.5
Outputs:
- excitation: bfloat16 [10656, 2048], P('col', 'row')
All inputs are finite; a program needn't handle non-finite values.
Results may differ from a plain program's by a relative error of at most 0.006.
Values may be sent and summed in bfloat16 or wider, within the bound.
A program may use at most 128 MiB of HBM per device.

v0:
```python
import jax
import jax.numpy as jnp
import numpy as np
from jax import lax
from jax.sharding import PartitionSpec as P

LDEG = 72
ITERS = 2


def angular_tables(degree):
    lat_count = 2 * degree
    lon_count = 4 * degree
    freq_count = 2 * degree + 1
    colatitude = (np.arange(lat_count) + 0.5) * np.pi / lat_count
    cos_col = np.cos(colatitude)
    sin_col = np.sin(colatitude)
    legendre = np.zeros((freq_count, degree, lat_count))
    diagonal_term = np.full(lat_count, np.sqrt(0.5))
    for order_m in range(degree + 1):
        if order_m > 0:
            diagonal_term = (
                diagonal_term * np.sqrt((2.0 * order_m + 1.0) / (2.0 * order_m)) * sin_col
            )
        earlier = np.zeros(lat_count)
        latest = diagonal_term
        for degree_l in range(order_m, degree + 1):
            if degree_l == order_m:
                current = diagonal_term
            elif degree_l == order_m + 1:
                current = np.sqrt(2.0 * order_m + 3.0) * cos_col * diagonal_term
            else:
                factor_a = np.sqrt((4.0 * degree_l**2 - 1.0) / (degree_l**2 - order_m**2))
                factor_b = np.sqrt(
                    ((degree_l - 1.0) ** 2 - order_m**2) / (4.0 * (degree_l - 1.0) ** 2 - 1.0)
                )
                current = factor_a * (cos_col * latest - factor_b * earlier)
            if degree_l > order_m:
                earlier, latest = (latest, current)
            if degree_l >= 1:
                legendre[order_m, degree_l - 1] = current
                if order_m >= 1:
                    legendre[degree + order_m, degree_l - 1] = current
    longitude = 2.0 * np.pi * np.arange(lon_count) / lon_count
    fourier = np.zeros((freq_count, lon_count))
    fourier[0] = 1.0 / np.sqrt(2.0 * np.pi)
    for order_m in range(1, degree + 1):
        fourier[order_m] = np.cos(order_m * longitude) / np.sqrt(np.pi)
        fourier[degree + order_m] = np.sin(order_m * longitude) / np.sqrt(np.pi)
    weight = sin_col * (np.pi / lat_count) * (2.0 * np.pi / lon_count)
    return (legendre, fourier, weight)


def level_skips(degree):
    skips = []
    for freq_index in range(2 * degree + 1):
        order_m = freq_index if freq_index <= degree else freq_index - degree
        skips.append(max(order_m - 1, 0))
    return skips


def spread_levels(halves, degree):
    columns = halves.shape[2]
    pieces = []
    start = 0
    for skip in level_skips(degree):
        count = degree - skip
        if skip > 0:
            pieces.append(jnp.zeros((2, skip, columns), halves.dtype))
        pieces.append(halves[:, start : start + count, :])
        start = start + count
    return jnp.concatenate(pieces, axis=1).reshape(2, 2 * degree + 1, degree, columns)


def pick_levels(projected, degree):
    pieces = []
    for freq_index, skip in enumerate(level_skips(degree)):
        pieces.append(projected[:, freq_index, skip:, :])
    return jnp.concatenate(pieces, axis=1)


def contrast_apply(coefficients, contrast, degree):
    legendre, fourier, weight = angular_tables(degree)
    legendre_wide = jnp.asarray(legendre, jnp.float32)
    legendre_narrow = jnp.asarray(legendre, jnp.bfloat16)
    fourier = jnp.asarray(fourier, jnp.float32)
    weight = jnp.asarray(weight, jnp.float32)
    columns = coefficients.shape[1]
    halves = coefficients.astype(jnp.bfloat16).reshape(2, -1, columns)
    padded = spread_levels(halves, degree)
    triple = lax.Precision.HIGH
    latitude = jnp.einsum(
        "qlt,cqlk->cktq", legendre_narrow, padded, preferred_element_type=jnp.float32
    )
    surface = jnp.einsum(
        "cktq,qp->cktp", latitude, fourier, precision=triple, preferred_element_type=jnp.float32
    )
    polar = contrast[0] * surface[0] + contrast[1] * surface[1]
    azimuth = contrast[1] * surface[0] + contrast[2] * surface[1]
    weighted = jnp.stack([polar, azimuth]) * weight[:, None]
    spectrum = jnp.einsum(
        "cktp,qp->cktq", weighted, fourier, precision=triple, preferred_element_type=jnp.float32
    )
    projected = jnp.einsum(
        "qlt,cktq->cqlk",
        legendre_wide,
        spectrum,
        precision=triple,
        preferred_element_type=jnp.float32,
    )
    picked = pick_levels(projected, degree)
    return picked.reshape(-1, columns).astype(jnp.bfloat16)


def body(tmatrix, panel, contrast):
    row_count = lax.axis_size("row")
    col_count = lax.axis_size("col")
    per_device = panel.shape[1] // col_count
    local_rows = tmatrix.shape[0]
    current = panel
    for iteration in range(ITERS):
        partial_value = jnp.dot(
            tmatrix,
            lax.all_gather(current, "row", axis=1, tiled=True),
            preferred_element_type=jnp.float32,
        )
        grouped = partial_value.reshape(local_rows, row_count, col_count, per_device)
        regrouped = lax.all_to_all(
            grouped.astype(jnp.bfloat16), "row", split_axis=1, concat_axis=0, tiled=True
        )
        summed = lax.psum_scatter(
            regrouped.astype(jnp.float32).astype(jnp.bfloat16),
            "col",
            scatter_dimension=2,
            tiled=True,
        )
        coupled = contrast_apply(summed.reshape(summed.shape[0], summed.shape[3]), contrast, LDEG)
        full_rows = coupled.shape[0]
        returned = lax.all_to_all(
            coupled.reshape(col_count, full_rows // col_count, 1, per_device),
            "col",
            split_axis=0,
            concat_axis=2,
            tiled=True,
        )
        returned = returned.reshape(full_rows // col_count, col_count * per_device)
        current = (panel.astype(jnp.float32) + returned.astype(jnp.float32)).astype(jnp.bfloat16)
    return current


def solution(mesh):
    placed = (P("row", "col"), P("col", "row"), P())
    return jax.shard_map(
        body, mesh=mesh, in_specs=placed, out_specs=P("col", "row"), check_vma=False
    )
```

profile of v0, /device:TPU:1, one launch (start us, length us, event | category | flops | bytes accessed | tf_op | source)
XLA Modules:
  0.0 546.1 jit_solution(4269901004636810020)
XLA Ops:
  6.5 0.7 all-gather.3.cloned.1.call-update
  7.3 68.5 %all-gather.3.cloned.1.call-done = bf16[1332,2048]{1,0:T(8,128)(2,1)} async-done(((bf16[1332,128]{1,0:T(8,128)(2,1)}), bf16[1332,2048]{1,0:T(8,128)(2,1)}) %all-gather.3.cloned.1.call-update) | async-done | bytes 5455888 | tf_op jit(solution)/shard_map/all_gather | solution.py:124
  75.8 8.5 %convolution_convert_fusion.1 = bf16[666,2048]{1,0:T(8,128)(2,1)} fusion(bf16[666,1332]{1,0:T(8,128)(2,1)S(1)} %copy-done, bf16[1332,2048]{1,0:T(8,128)(2,1)} %all-gather.3.cloned.1.call-done), kind=kOutput, calls=%fused_computation.19 | convolution fusion | flops 3634974720 | bytes 9958032 | tf_op jit(solution)/shard_map/dot_general | solution.py:122
  84.2 4.7 copy.125
  88.9 42.1 %all_to_all.54 = bf16[666,16,8,16]{0,3,2,1:T(8,128)(2,1)S(1)} all-to-all(bf16[666,16,8,16]{0,3,2,1:T(8,128)(2,1)} %bitcast.665), channel_id=1, replica_groups=mesh['row'=16,'col'=8] {'row'}, dimensions={1} | all-to-all | bytes 5455872 | tf_op jit(solution)/shard_map/all_to_all | solution.py:128
  131.0 3.4 copy.126
  134.5 6.9 %all_to_all.43 = bf16[10656,1,8,16]{0,3,2,1:T(8,128)(2,1)} reshape(bf16[16,666,1,8,16]{1,0,4,3,2:T(8,128)(2,1)} %copy.126) | data formatting | bytes 5455872 | tf_op jit(solution)/shard_map/all_to_all | solution.py:128
  141.4 1.1 copy-done.10
  142.4 0.9 slice_bitcast_fusion.2
  143.3 30.5 %reduce-scatter.3.cloned.1.call-done = bf16[10656,1,1,16]{0,3,2,1:T(8,128)(2,1)} async-done(((bf16[10656,1,8,16]{0,3,2,1:T(8,128)(2,1)}), bf16[10656,1,1,16]{0,3,2,1:T(8,128)(2,1)}) %reduce-scatter.3.cloned.1.call-update) | async-done | bytes 341008 | tf_op jit(solution)/shard_map/reduce_scatter | solution.py:131
  173.8 1.3 reshape_reshape.6
  181.1 0.7 fusion.104
  181.8 0.7 fusion.105
  183.9 0.7 fusion.108
  186.7 0.7 fusion.112
  187.4 0.7 fusion.113
  188.1 0.7 fusion.114
  188.8 0.7 fusion.115
  189.5 0.7 fusion.116
  190.2 0.7 fusion.117
  193.6 0.7 fusion.122
  194.3 0.7 fusion.123
  195.0 0.7 fusion.124
  195.7 0.7 fusion.125
  196.4 0.7 fusion.126
  199.2 0.7 fusion.130
  199.9 0.7 fusion.131
  200.6 0.7 fusion.132
  209.8 1.6 concatenate.24
  212.7 11.8 %concatenate.23 = bf16[2,9417,16]{1,0,2:T(2,128)(2,1)S(1)} concatenate(bf16[2,144,16]{1,0,2:T(2,128)(2,1)S(1)} %slice.2639, bf16[2,1,16]{1,0,2:T(2,128)(2,1)S(1)} %broadcast.223, bf16[2,71,16]{1,0,2:T(2,128)(2,1)} %get-tuple-element.457, bf16[2,2,16]{1,0,2:T(2,128)(2,1)S(1)} %broadcast.224, bf16[2,70,16]{1,0,2:T(2,128)(2,1)} %get-tuple-element.455, ...), dimensions={1} | concatenate | bytes 1205376
  224.9 1.5 pad_maximum_fusion
  226.4 3.7 reshape.59
  230.1 3.5 convolution_bitcast_fusion.1
  233.7 7.1 %fusion.8 = f32[2,16,144,288]{3,2,1,0:T(8,128)S(1)} fusion(f32[145,288,1,1]{1,0,3,2:T(8,128)S(1)} %copy-done.2, f32[2,16,144,145]{2,1,0,3:T(8,128)S(1)} %convolution_bitcast_fusion.1), kind=kOutput, calls=%fused_computation.10 | convolution fusion | flops 1154580480 | bytes 8148096 | tf_op jit(solution)/shard_map/cktq,qp->cktp/dot_general | solution.py:95
  240.9 0.7 multiply_add_fusion.3
  241.6 5.6 %fusion = f32[2,16,144,145]{3,2,1,0:T(8,128)} fusion(f32[145,288,1,1]{1,0,3,2:T(8,128)S(1)} %copy-done.2, f32[1,16,144,288]{3,2,1,0:T(8,128)S(1)} %get-tuple-element.8, f32[1,16,144,288]{3,2,1,0:T(8,128)S(1)} %get-tuple-element.7, f32[144]{0:T(256)S(1)} %copy-done.89), kind=kOutput, calls=%fused_computation.1 | convolution fusion | flops 1157234688 | bytes 8148672 | tf_op jit(solution)/shard_map/cktp,qp->cktq/dot_general | solution.py:101
  247.3 6.8 %copy.130 = f32[2,16,144,145]{2,1,0,3:T(8,128)} copy(f32[2,16,144,145]{3,2,1,0:T(8,128)} %fusion) | data formatting | bytes 5345280 | tf_op jit(solution)/shard_map/cktp,qp->cktq/dot_general | solution.py:101
  254.1 9.8 %fusion.13 = bf16[2,145,72,16]{2,3,0,1:T(8,128)(2,1)S(1)} fusion(f32[2,16,144,145]{2,1,0,3:T(8,128)} %copy.130, f32[145,72,144,1]{2,1,3,0:T(8,128)} %constant.13), kind=kOutput, calls=%fused_computation.25 | convolution fusion | flops 288979200 | bytes 9354240 | tf_op jit(solution)/shard_map/qlt,cktq->cqlk/dot_general | solution.py:104
  280.2 1.5 concatenate.17
  282.3 0.8 copy.146
  283.1 7.7 %all-to-all-start.1 = ((bf16[8,1332,1,16]{1,3,2,0:T(8,128)(2,1)}), bf16[8,1332,1,16]{1,3,2,0:T(8,128)(2,1)}, u32[]{:S(2)}, u32[]{:S(2)}) async-start(bf16[8,1332,1,16]{1,3,2,0:T(8,128)(2,1)} %copy.146), calls=%async_computation.2 | async-start | bytes 720896 | tf_op jit(solution)/shard_map/all_to_all | solution.py:139
  290.9 7.6 %all-to-all-done.1 = bf16[8,1332,1,16]{1,3,2,0:T(8,128)(2,1)} async-done(((bf16[8,1332,1,16]{1,3,2,0:T(8,128)(2,1)}), bf16[8,1332,1,16]{1,3,2,0:T(8,128)(2,1)}, u32[]{:S(2)}, u32[]{:S(2)}) %all-to-all-start.1) | async-done | bytes 341024 | tf_op jit(solution)/shard_map/all_to_all | solution.py:139
  298.6 1.0 bitcast_convert_fusion.1
  299.6 0.8 fusion.17
  300.5 58.7 %all-gather.5.cloned.1.call-done = bf16[1332,2048]{0,1:T(8,128)(2,1)} async-done(((bf16[1332,128]{0,1:T(8,128)(2,1)}), bf16[1332,2048]{0,1:T(8,128)(2,1)}) %all-gather.5.cloned.1.call-update) | async-done | bytes 5455888 | tf_op jit(solution)/shard_map/all_gather | solution.py:124
  359.2 8.5 %fusion.12 = bf16[666,2048]{1,0:T(8,128)(2,1)} fusion(bf16[1332,2048]{0,1:T(8,128)(2,1)} %all-gather.5.cloned.1.call-done, bf16[666,1332]{1,0:T(8,128)(2,1)S(1)} %copy-done), kind=kOutput, calls=%fused_computation.20 | convolution fusion | flops 3634974720 | bytes 9958032 | tf_op jit(solution)/shard_map/dot_general | solution.py:122
  367.7 4.7 copy.147
  372.3 43.1 %all_to_all.55 = bf16[666,16,8,16]{0,3,2,1:T(8,128)(2,1)S(1)} all-to-all(bf16[666,16,8,16]{0,3,2,1:T(8,128)(2,1)} %bitcast.667), channel_id=1, replica_groups=mesh['row'=16,'col'=8] {'row'}, dimensions={1} | all-to-all | bytes 5455872 | tf_op jit(solution)/shard_map/all_to_all | solution.py:128
  415.4 3.4 copy.148
  418.8 6.9 %all_to_all.48 = bf16[10656,1,8,16]{0,3,2,1:T(8,128)(2,1)} reshape(bf16[16,666,1,8,16]{1,0,4,3,2:T(8,128)(2,1)} %copy.148) | data formatting | bytes 5455872 | tf_op jit(solution)/shard_map/all_to_all | solution.py:128
  425.7 32.3 %reduce-scatter.5.cloned.1.call-done = bf16[10656,1,1,16]{0,3,2,1:T(8,128)(2,1)} async-done(((bf16[10656,1,8,16]{0,3,2,1:T(8,128)(2,1)}), bf16[10656,1,1,16]{0,3,2,1:T(8,128)(2,1)}) %reduce-scatter.5.cloned.1.call-update) | async-done | bytes 341008 | tf_op jit(solution)/shard_map/reduce_scatter | solution.py:131
  458.0 1.3 reshape_reshape.7
  467.4 1.6 concatenate.21
  469.3 9.9 %concatenate.20 = bf16[2,9417,16]{1,0,2:T(2,128)(2,1)S(1)} concatenate(bf16[2,144,16]{1,0,2:T(2,128)(2,1)S(1)} %slice.2929, bf16[2,1,16]{1,0,2:T(2,128)(2,1)S(1)} %broadcast.223, bf16[2,71,16]{1,0,2:T(2,128)(2,1)S(1)} %get-tuple-element.345, bf16[2,2,16]{1,0,2:T(2,128)(2,1)S(1)} %broadcast.224, bf16[2,70,16]{1,0,2:T(2,128)(2,1)S(1)} %get-tuple-element.343, ...), dimensions={1} | concatenate | bytes 1205376
  479.9 2.0 reshape.60
  482.0 3.5 convolution_bitcast_fusion
  485.5 7.1 %fusion.6 = f32[2,16,144,288]{3,2,1,0:T(8,128)S(1)} fusion(f32[145,288,1,1]{1,0,3,2:T(8,128)S(1)} %copy-done.2, f32[2,16,144,145]{2,1,0,3:T(8,128)S(1)} %convolution_bitcast_fusion), kind=kOutput, calls=%fused_computation.8 | convolution fusion | flops 1154580480 | bytes 8148096 | tf_op jit(solution)/shard_map/cktq,qp->cktp/dot_general | solution.py:95
  492.7 0.7 multiply_add_fusion.1
  493.4 5.9 %fusion.3 = f32[2,16,144,145]{3,2,1,0:T(8,128)} fusion(f32[145,288,1,1]{1,0,3,2:T(8,128)S(1)} %copy-done.2, f32[1,16,144,288]{3,2,1,0:T(8,128)S(1)} %get-tuple-element.6, f32[1,16,144,288]{3,2,1,0:T(8,128)S(1)} %get-tuple-element.5, f32[144]{0:T(256)S(1)} %copy-done.89), kind=kOutput, calls=%fused_computation.5 | convolution fusion | flops 1157234688 | bytes 8148672 | tf_op jit(solution)/shard_map/cktp,qp->cktq/dot_general | solution.py:101
  499.3 6.4 %copy.152 = f32[2,16,144,145]{2,1,0,3:T(8,128)} copy(f32[2,16,144,145]{3,2,1,0:T(8,128)} %fusion.3) | data formatting | bytes 5345280 | tf_op jit(solution)/shard_map/cktp,qp->cktq/dot_general | solution.py:101
  505.7 9.8 %fusion.14 = bf16[2,145,72,16]{2,3,0,1:T(8,128)(2,1)S(1)} fusion(f32[2,16,144,145]{2,1,0,3:T(8,128)} %copy.152, f32[145,72,144,1]{2,1,3,0:T(8,128)} %constant.13), kind=kOutput, calls=%fused_computation.26 | convolution fusion | flops 288979200 | bytes 9354240 | tf_op jit(solution)/shard_map/qlt,cktq->cqlk/dot_general | solution.py:104
  522.3 0.9 concatenate.19
  523.8 13.8 %all_to_all.56 = bf16[8,1332,1,16]{1,3,2,0:T(8,128)(2,1)S(1)} all-to-all(bf16[8,1332,1,16]{1,3,2,0:T(8,128)(2,1)S(1)} %copy.168), channel_id=1, replica_groups=mesh['row'=16,'col'=8] {'col'}, dimensions={0} | all-to-all | bytes 681984 | tf_op jit(solution)/shard_map/all_to_all | solution.py:139
  537.8 0.9 copy.169
  (584 shorter events, 56.7 us)
Async XLA Ops:
  6.5 69.2 %copy-start = (bf16[666,1332]{1,0:T(8,128)(2,1)S(1)}, bf16[666,1332]{1,0:T(8,128)(2,1)}, u32[]{:S(2)}) copy-start(bf16[666,1332]{1,0:T(8,128)(2,1)} %param.11) | copy-start | bytes 5322676
  6.5 69.2 %all-gather.3.cloned.1.call-start = ((), (), s32[]{:S(2)}) async-start(), calls=%async_computation.6 | async-start | bytes 5814272 | tf_op jit(solution)/shard_map/all_gather | solution.py:124
  7.3 166.5 %reduce-scatter.3.cloned.1.call-start = ((), (), s32[]{:S(2)}) async-start(), calls=%async_computation.7 | async-start | bytes 3096576 | tf_op jit(solution)/shard_map/reduce_scatter | solution.py:131
  203.8 20.8 %copy-start.81 = (bf16[2,58,16]{1,0,2:T(2,128)(2,1)}, bf16[2,58,16]{1,0,2:T(2,128)(2,1)S(1)}, u32[]{:S(2)}) copy-start(bf16[2,58,16]{1,0,2:T(2,128)(2,1)S(1)} %broadcast.280) | copy-start | bytes 11140
  203.8 20.7 %copy-start.83 = (bf16[2,59,16]{1,0,2:T(2,128)(2,1)}, bf16[2,59,16]{1,0,2:T(2,128)(2,1)S(1)}, u32[]{:S(2)}) copy-start(bf16[2,59,16]{1,0,2:T(2,128)(2,1)S(1)} %broadcast.281) | copy-start | bytes 11332
  203.8 20.7 %copy-start.85 = (bf16[2,60,16]{1,0,2:T(2,128)(2,1)}, bf16[2,60,16]{1,0,2:T(2,128)(2,1)S(1)}, u32[]{:S(2)}) copy-start(bf16[2,60,16]{1,0,2:T(2,128)(2,1)S(1)} %broadcast.282) | copy-start | bytes 11524
  203.8 20.7 %copy-start.87 = (bf16[2,61,16]{1,0,2:T(2,128)(2,1)}, bf16[2,61,16]{1,0,2:T(2,128)(2,1)S(1)}, u32[]{:S(2)}) copy-start(bf16[2,61,16]{1,0,2:T(2,128)(2,1)S(1)} %broadcast.283) | copy-start | bytes 11716
  211.8 12.7 %copy-start.11 = (bf16[2,23,16]{1,0,2:T(2,128)(2,1)}, bf16[2,23,16]{1,0,2:T(2,128)(2,1)S(1)}, u32[]{:S(2)}) copy-start(bf16[2,23,16]{1,0,2:T(2,128)(2,1)S(1)} %broadcast.245) | copy-start | bytes 4420
  211.8 12.7 %copy-start.13 = (bf16[2,24,16]{1,0,2:T(2,128)(2,1)}, bf16[2,24,16]{1,0,2:T(2,128)(2,1)S(1)}, u32[]{:S(2)}) copy-start(bf16[2,24,16]{1,0,2:T(2,128)(2,1)S(1)} %broadcast.246) | copy-start | bytes 4612
  211.9 12.7 %copy-start.15 = (bf16[2,25,16]{1,0,2:T(2,128)(2,1)}, bf16[2,25,16]{1,0,2:T(2,128)(2,1)S(1)}, u32[]{:S(2)}) copy-start(bf16[2,25,16]{1,0,2:T(2,128)(2,1)S(1)} %broadcast.247) | copy-start | bytes 4804
  211.9 12.7 %copy-start.17 = (bf16[2,26,16]{1,0,2:T(2,128)(2,1)}, bf16[2,26,16]{1,0,2:T(2,128)(2,1)S(1)}, u32[]{:S(2)}) copy-start(bf16[2,26,16]{1,0,2:T(2,128)(2,1)S(1)} %broadcast.248) | copy-start | bytes 4996
  211.9 12.7 %copy-start.19 = (bf16[2,27,16]{1,0,2:T(2,128)(2,1)}, bf16[2,27,16]{1,0,2:T(2,128)(2,1)S(1)}, u32[]{:S(2)}) copy-start(bf16[2,27,16]{1,0,2:T(2,128)(2,1)S(1)} %broadcast.249) | copy-start | bytes 5188
  211.9 12.7 %copy-start.21 = (bf16[2,28,16]{1,0,2:T(2,128)(2,1)}, bf16[2,28,16]{1,0,2:T(2,128)(2,1)S(1)}, u32[]{:S(2)}) copy-start(bf16[2,28,16]{1,0,2:T(2,128)(2,1)S(1)} %broadcast.250) | copy-start | bytes 5380
  211.9 12.7 %copy-start.23 = (bf16[2,29,16]{1,0,2:T(2,128)(2,1)}, bf16[2,29,16]{1,0,2:T(2,128)(2,1)S(1)}, u32[]{:S(2)}) copy-start(bf16[2,29,16]{1,0,2:T(2,128)(2,1)S(1)} %broadcast.251) | copy-start | bytes 5572
  212.0 12.6 %copy-start.25 = (bf16[2,30,16]{1,0,2:T(2,128)(2,1)}, bf16[2,30,16]{1,0,2:T(2,128)(2,1)S(1)}, u32[]{:S(2)}) copy-start(bf16[2,30,16]{1,0,2:T(2,128)(2,1)S(1)} %broadcast.252) | copy-start | bytes 5764
  212.0 12.6 %copy-start.27 = (bf16[2,31,16]{1,0,2:T(2,128)(2,1)}, bf16[2,31,16]{1,0,2:T(2,128)(2,1)S(1)}, u32[]{:S(2)}) copy-start(bf16[2,31,16]{1,0,2:T(2,128)(2,1)S(1)} %broadcast.253) | copy-start | bytes 5956
  212.0 12.6 %copy-start.29 = (bf16[2,32,16]{1,0,2:T(2,128)(2,1)}, bf16[2,32,16]{1,0,2:T(2,128)(2,1)S(1)}, u32[]{:S(2)}) copy-start(bf16[2,32,16]{1,0,2:T(2,128)(2,1)S(1)} %broadcast.254) | copy-start | bytes 6148
  212.0 12.6 %copy-start.31 = (bf16[2,33,16]{1,0,2:T(2,128)(2,1)}, bf16[2,33,16]{1,0,2:T(2,128)(2,1)S(1)}, u32[]{:S(2)}) copy-start(bf16[2,33,16]{1,0,2:T(2,128)(2,1)S(1)} %broadcast.255) | copy-start | bytes 6340
  212.1 12.6 %copy-start.33 = (bf16[2,34,16]{1,0,2:T(2,128)(2,1)}, bf16[2,34,16]{1,0,2:T(2,128)(2,1)S(1)}, u32[]{:S(2)}) copy-start(bf16[2,34,16]{1,0,2:T(2,128)(2,1)S(1)} %broadcast.256) | copy-start | bytes 6532
  212.1 12.6 %copy-start.35 = (bf16[2,35,16]{1,0,2:T(2,128)(2,1)}, bf16[2,35,16]{1,0,2:T(2,128)(2,1)S(1)}, u32[]{:S(2)}) copy-start(bf16[2,35,16]{1,0,2:T(2,128)(2,1)S(1)} %broadcast.257) | copy-start | bytes 6724
  212.1 12.6 %copy-start.37 = (bf16[2,36,16]{1,0,2:T(2,128)(2,1)}, bf16[2,36,16]{1,0,2:T(2,128)(2,1)S(1)}, u32[]{:S(2)}) copy-start(bf16[2,36,16]{1,0,2:T(2,128)(2,1)S(1)} %broadcast.258) | copy-start | bytes 6916
  212.1 12.5 %copy-start.39 = (bf16[2,37,16]{1,0,2:T(2,128)(2,1)}, bf16[2,37,16]{1,0,2:T(2,128)(2,1)S(1)}, u32[]{:S(2)}) copy-start(bf16[2,37,16]{1,0,2:T(2,128)(2,1)S(1)} %broadcast.259) | copy-start | bytes 7108
  212.2 12.5 %copy-start.41 = (bf16[2,38,16]{1,0,2:T(2,128)(2,1)}, bf16[2,38,16]{1,0,2:T(2,128)(2,1)S(1)}, u32[]{:S(2)}) copy-start(bf16[2,38,16]{1,0,2:T(2,128)(2,1)S(1)} %broadcast.260) | copy-start | bytes 7300
  212.2 12.5 %copy-start.43 = (bf16[2,39,16]{1,0,2:T(2,128)(2,1)}, bf16[2,39,16]{1,0,2:T(2,128)(2,1)S(1)}, u32[]{:S(2)}) copy-start(bf16[2,39,16]{1,0,2:T(2,128)(2,1)S(1)} %broadcast.261) | copy-start | bytes 7492
  212.2 12.5 %copy-start.45 = (bf16[2,40,16]{1,0,2:T(2,128)(2,1)}, bf16[2,40,16]{1,0,2:T(2,128)(2,1)S(1)}, u32[]{:S(2)}) copy-start(bf16[2,40,16]{1,0,2:T(2,128)(2,1)S(1)} %broadcast.262) | copy-start | bytes 7684
  212.2 12.5 %copy-start.47 = (bf16[2,41,16]{1,0,2:T(2,128)(2,1)}, bf16[2,41,16]{1,0,2:T(2,128)(2,1)S(1)}, u32[]{:S(2)}) copy-start(bf16[2,41,16]{1,0,2:T(2,128)(2,1)S(1)} %broadcast.263) | copy-start | bytes 7876
  212.3 12.5 %copy-start.49 = (bf16[2,42,16]{1,0,2:T(2,128)(2,1)}, bf16[2,42,16]{1,0,2:T(2,128)(2,1)S(1)}, u32[]{:S(2)}) copy-start(bf16[2,42,16]{1,0,2:T(2,128)(2,1)S(1)} %broadcast.264) | copy-start | bytes 8068
  212.3 12.5 %copy-start.51 = (bf16[2,43,16]{1,0,2:T(2,128)(2,1)}, bf16[2,43,16]{1,0,2:T(2,128)(2,1)S(1)}, u32[]{:S(2)}) copy-start(bf16[2,43,16]{1,0,2:T(2,128)(2,1)S(1)} %broadcast.265) | copy-start | bytes 8260
  212.3 12.4 %copy-start.53 = (bf16[2,44,16]{1,0,2:T(2,128)(2,1)}, bf16[2,44,16]{1,0,2:T(2,128)(2,1)S(1)}, u32[]{:S(2)}) copy-start(bf16[2,44,16]{1,0,2:T(2,128)(2,1)S(1)} %broadcast.266) | copy-start | bytes 8452
  212.3 12.4 %copy-start.55 = (bf16[2,45,16]{1,0,2:T(2,128)(2,1)}, bf16[2,45,16]{1,0,2:T(2,128)(2,1)S(1)}, u32[]{:S(2)}) copy-start(bf16[2,45,16]{1,0,2:T(2,128)(2,1)S(1)} %broadcast.267) | copy-start | bytes 8644
  212.4 12.4 %copy-start.57 = (bf16[2,46,16]{1,0,2:T(2,128)(2,1)}, bf16[2,46,16]{1,0,2:T(2,128)(2,1)S(1)}, u32[]{:S(2)}) copy-start(bf16[2,46,16]{1,0,2:T(2,128)(2,1)S(1)} %broadcast.268) | copy-start | bytes 8836
  212.4 12.4 %copy-start.59 = (bf16[2,47,16]{1,0,2:T(2,128)(2,1)}, bf16[2,47,16]{1,0,2:T(2,128)(2,1)S(1)}, u32[]{:S(2)}) copy-start(bf16[2,47,16]{1,0,2:T(2,128)(2,1)S(1)} %broadcast.269) | copy-start | bytes 9028
  212.4 12.4 %copy-start.61 = (bf16[2,48,16]{1,0,2:T(2,128)(2,1)}, bf16[2,48,16]{1,0,2:T(2,128)(2,1)S(1)}, u32[]{:S(2)}) copy-start(bf16[2,48,16]{1,0,2:T(2,128)(2,1)S(1)} %broadcast.270) | copy-start | bytes 9220
  212.4 12.4 %copy-start.63 = (bf16[2,49,16]{1,0,2:T(2,128)(2,1)}, bf16[2,49,16]{1,0,2:T(2,128)(2,1)S(1)}, u32[]{:S(2)}) copy-start(bf16[2,49,16]{1,0,2:T(2,128)(2,1)S(1)} %broadcast.271) | copy-start | bytes 9412
  212.5 12.3 %copy-start.65 = (bf16[2,50,16]{1,0,2:T(2,128)(2,1)}, bf16[2,50,16]{1,0,2:T(2,128)(2,1)S(1)}, u32[]{:S(2)}) copy-start(bf16[2,50,16]{1,0,2:T(2,128)(2,1)S(1)} %broadcast.272) | copy-start | bytes 9604
  212.5 12.3 %copy-start.67 = (bf16[2,51,16]{1,0,2:T(2,128)(2,1)}, bf16[2,51,16]{1,0,2:T(2,128)(2,1)S(1)}, u32[]{:S(2)}) copy-start(bf16[2,51,16]{1,0,2:T(2,128)(2,1)S(1)} %broadcast.273) | copy-start | bytes 9796
  212.5 12.3 %copy-start.69 = (bf16[2,52,16]{1,0,2:T(2,128)(2,1)}, bf16[2,52,16]{1,0,2:T(2,128)(2,1)S(1)}, u32[]{:S(2)}) copy-start(bf16[2,52,16]{1,0,2:T(2,128)(2,1)S(1)} %broadcast.274) | copy-start | bytes 9988
  212.5 12.3 %copy-start.71 = (bf16[2,53,16]{1,0,2:T(2,128)(2,1)}, bf16[2,53,16]{1,0,2:T(2,128)(2,1)S(1)}, u32[]{:S(2)}) copy-start(bf16[2,53,16]{1,0,2:T(2,128)(2,1)S(1)} %broadcast.275) | copy-start | bytes 10180
  212.6 12.3 %copy-start.73 = (bf16[2,54,16]{1,0,2:T(2,128)(2,1)}, bf16[2,54,16]{1,0,2:T(2,128)(2,1)S(1)}, u32[]{:S(2)}) copy-start(bf16[2,54,16]{1,0,2:T(2,128)(2,1)S(1)} %broadcast.276) | copy-start | bytes 10372
  212.6 12.3 %copy-start.75 = (bf16[2,55,16]{1,0,2:T(2,128)(2,1)}, bf16[2,55,16]{1,0,2:T(2,128)(2,1)S(1)}, u32[]{:S(2)}) copy-start(bf16[2,55,16]{1,0,2:T(2,128)(2,1)S(1)} %broadcast.277) | copy-start | bytes 10564
  212.6 12.3 %copy-start.77 = (bf16[2,56,16]{1,0,2:T(2,128)(2,1)}, bf16[2,56,16]{1,0,2:T(2,128)(2,1)S(1)}, u32[]{:S(2)}) copy-start(bf16[2,56,16]{1,0,2:T(2,128)(2,1)S(1)} %broadcast.278) | copy-start | bytes 10756
  212.6 12.2 %copy-start.79 = (bf16[2,57,16]{1,0,2:T(2,128)(2,1)}, bf16[2,57,16]{1,0,2:T(2,128)(2,1)S(1)}, u32[]{:S(2)}) copy-start(bf16[2,57,16]{1,0,2:T(2,128)(2,1)S(1)} %broadcast.279) | copy-start | bytes 10948
  281.9 8.8 %copy-start.9 = (bf16[1332,128]{1,0:T(8,128)(2,1)S(1)}, bf16[1332,128]{1,0:T(8,128)(2,1)}, u32[]{:S(2)}) copy-start(bf16[1332,128]{1,0:T(8,128)(2,1)} %param.12) | copy-start | bytes 1022980
  283.1 15.5 %all-to-all-start.1 = ((bf16[8,1332,1,16]{1,3,2,0:T(8,128)(2,1)}), bf16[8,1332,1,16]{1,3,2,0:T(8,128)(2,1)}, u32[]{:S(2)}, u32[]{:S(2)}) async-start(bf16[8,1332,1,16]{1,3,2,0:T(8,128)(2,1)} %copy.146), calls=%async_computation.2 | async-start | bytes 720896 | tf_op jit(solution)/shard_map/all_to_all | solution.py:139
  290.7 68.5 %all-gather.5.cloned.1.call-start = ((), (), s32[]{:S(2)}) async-start(), calls=%async_computation.8 | async-start | bytes 6127616 | tf_op jit(solution)/shard_map/all_gather | solution.py:124
  300.4 157.6 %reduce-scatter.5.cloned.1.call-start = ((), (), s32[]{:S(2)}) async-start(), calls=%async_computation.9 | async-start | bytes 3096576 | tf_op jit(solution)/shard_map/reduce_scatter | solution.py:131
  460.7 8.3 %copy-start.12 = (bf16[2,23,16]{1,0,2:T(2,128)(2,1)S(1)}, bf16[2,23,16]{1,0,2:T(2,128)(2,1)}, u32[]{:S(2)}) copy-start(bf16[2,23,16]{1,0,2:T(2,128)(2,1)} %copy-done.11) | copy-start | bytes 4420
  460.8 8.3 %copy-start.14 = (bf16[2,24,16]{1,0,2:T(2,128)(2,1)S(1)}, bf16[2,24,16]{1,0,2:T(2,128)(2,1)}, u32[]{:S(2)}) copy-start(bf16[2,24,16]{1,0,2:T(2,128)(2,1)} %copy-done.13) | copy-start | bytes 4612
  460.8 8.3 %copy-start.16 = (bf16[2,25,16]{1,0,2:T(2,128)(2,1)S(1)}, bf16[2,25,16]{1,0,2:T(2,128)(2,1)}, u32[]{:S(2)}) copy-start(bf16[2,25,16]{1,0,2:T(2,128)(2,1)} %copy-done.15) | copy-start | bytes 4804
  460.8 8.3 %copy-start.18 = (bf16[2,26,16]{1,0,2:T(2,128)(2,1)S(1)}, bf16[2,26,16]{1,0,2:T(2,128)(2,1)}, u32[]{:S(2)}) copy-start(bf16[2,26,16]{1,0,2:T(2,128)(2,1)} %copy-done.17) | copy-start | bytes 4996
  460.8 8.3 %copy-start.20 = (bf16[2,27,16]{1,0,2:T(2,128)(2,1)S(1)}, bf16[2,27,16]{1,0,2:T(2,128)(2,1)}, u32[]{:S(2)}) copy-start(bf16[2,27,16]{1,0,2:T(2,128)(2,1)} %copy-done.19) | copy-start | bytes 5188
  460.8 8.3 %copy-start.22 = (bf16[2,28,16]{1,0,2:T(2,128)(2,1)S(1)}, bf16[2,28,16]{1,0,2:T(2,128)(2,1)}, u32[]{:S(2)}) copy-start(bf16[2,28,16]{1,0,2:T(2,128)(2,1)} %copy-done.21) | copy-start | bytes 5380
  460.8 8.3 %copy-start.24 = (bf16[2,29,16]{1,0,2:T(2,128)(2,1)S(1)}, bf16[2,29,16]{1,0,2:T(2,128)(2,1)}, u32[]{:S(2)}) copy-start(bf16[2,29,16]{1,0,2:T(2,128)(2,1)} %copy-done.23) | copy-start | bytes 5572
  460.8 8.3 %copy-start.26 = (bf16[2,30,16]{1,0,2:T(2,128)(2,1)S(1)}, bf16[2,30,16]{1,0,2:T(2,128)(2,1)}, u32[]{:S(2)}) copy-start(bf16[2,30,16]{1,0,2:T(2,128)(2,1)} %copy-done.25) | copy-start | bytes 5764
  460.8 8.3 %copy-start.28 = (bf16[2,31,16]{1,0,2:T(2,128)(2,1)S(1)}, bf16[2,31,16]{1,0,2:T(2,128)(2,1)}, u32[]{:S(2)}) copy-start(bf16[2,31,16]{1,0,2:T(2,128)(2,1)} %copy-done.27) | copy-start | bytes 5956
  460.8 8.3 %copy-start.30 = (bf16[2,32,16]{1,0,2:T(2,128)(2,1)S(1)}, bf16[2,32,16]{1,0,2:T(2,128)(2,1)}, u32[]{:S(2)}) copy-start(bf16[2,32,16]{1,0,2:T(2,128)(2,1)} %copy-done.29) | copy-start | bytes 6148
  460.8 8.3 %copy-start.32 = (bf16[2,33,16]{1,0,2:T(2,128)(2,1)S(1)}, bf16[2,33,16]{1,0,2:T(2,128)(2,1)}, u32[]{:S(2)}) copy-start(bf16[2,33,16]{1,0,2:T(2,128)(2,1)} %copy-done.31) | copy-start | bytes 6340
  460.9 8.3 %copy-start.34 = (bf16[2,34,16]{1,0,2:T(2,128)(2,1)S(1)}, bf16[2,34,16]{1,0,2:T(2,128)(2,1)}, u32[]{:S(2)}) copy-start(bf16[2,34,16]{1,0,2:T(2,128)(2,1)} %copy-done.33) | copy-start | bytes 6532
  460.9 8.3 %copy-start.36 = (bf16[2,35,16]{1,0,2:T(2,128)(2,1)S(1)}, bf16[2,35,16]{1,0,2:T(2,128)(2,1)}, u32[]{:S(2)}) copy-start(bf16[2,35,16]{1,0,2:T(2,128)(2,1)} %copy-done.35) | copy-start | bytes 6724
  460.9 8.3 %copy-start.38 = (bf16[2,36,16]{1,0,2:T(2,128)(2,1)S(1)}, bf16[2,36,16]{1,0,2:T(2,128)(2,1)}, u32[]{:S(2)}) copy-start(bf16[2,36,16]{1,0,2:T(2,128)(2,1)} %copy-done.37) | copy-start | bytes 6916
  460.9 8.3 %copy-start.40 = (bf16[2,37,16]{1,0,2:T(2,128)(2,1)S(1)}, bf16[2,37,16]{1,0,2:T(2,128)(2,1)}, u32[]{:S(2)}) copy-start(bf16[2,37,16]{1,0,2:T(2,128)(2,1)} %copy-done.39) | copy-start | bytes 7108
  460.9 8.3 %copy-start.42 = (bf16[2,38,16]{1,0,2:T(2,128)(2,1)S(1)}, bf16[2,38,16]{1,0,2:T(2,128)(2,1)}, u32[]{:S(2)}) copy-start(bf16[2,38,16]{1,0,2:T(2,128)(2,1)} %copy-done.41) | copy-start | bytes 7300
  460.9 8.3 %copy-start.44 = (bf16[2,39,16]{1,0,2:T(2,128)(2,1)S(1)}, bf16[2,39,16]{1,0,2:T(2,128)(2,1)}, u32[]{:S(2)}) copy-start(bf16[2,39,16]{1,0,2:T(2,128)(2,1)} %copy-done.43) | copy-start | bytes 7492
  460.9 8.3 %copy-start.46 = (bf16[2,40,16]{1,0,2:T(2,128)(2,1)S(1)}, bf16[2,40,16]{1,0,2:T(2,128)(2,1)}, u32[]{:S(2)}) copy-start(bf16[2,40,16]{1,0,2:T(2,128)(2,1)} %copy-done.45) | copy-start | bytes 7684
  (31 other events, 222.3 us)
Sparse Core Ops, SparseCore 0:
  9.5 66.2 all-gather.2
  141.5 32.2 reduce-scatter.2
  300.5 58.5 all-gather.4
  425.8 32.1 reduce-scatter.4
where the time goes:
time: 550 us; the launch traced here: 546 us
  waiting for transfers between devices  198 us (36%)
  local copies, waits for them, and re-layouts  150 us (27%)
  blocking collectives  99 us (18%)
  matrix products  69.4 us (13%)
  between operations  15.9 us (3%)
  starting transfers between devices  7.75 us (1%)
  other arithmetic  5.58 us (1%)
    all_gather x2, waiting for transfers between devices, body(): lax.all_gather(current, 'row', axis=1, tiled=True)  127 us
    all_to_all x2, blocking collectives, body(): lax.all_to_all(grouped.astype(jnp.bfloat16), 'row', split_axis=1, concat_...  85.2 us
    reduce_scatter x2, waiting for transfers between devices, body(): lax.psum_scatter(regrouped.astype(jnp.float32).astype(jnp.bfloat16), 'col...  62.8 us
    slice x174, local copies, waits for them, and re-layouts, spread_levels(): pieces.append(halves[:, start:start + count, :])  35.8 us
    unnamed x185, local copies, waits for them, and re-layouts  27.3 us
    squeeze x161, local copies, waits for them, and re-layouts, pick_levels(): pieces.append(projected[:, freq_index, skip:, :])  22.9 us
    all_to_all x4, local copies, waits for them, and re-layouts, body(): lax.all_to_all(grouped.astype(jnp.bfloat16), 'row', split_axis=1, concat_...  20.6 us
    dot_general x2, matrix products, contrast_apply(): jnp.einsum('qlt,cktq->cqlk', legendre_wide, spectrum, precision=triple, p...  19.7 us
  transfers between devices with their start and end apart: 5, of which 5 were waited for; matrix products, arithmetic and copies ran while one was open for 0% of the time, Pallas kernels for 0%

commit v1 on v0

--- a/solution.py
+++ b/solution.py
@@ -121,7 +121,9 @@
     for iteration in range(ITERS):
         partial_value = jnp.dot(
             tmatrix,
-            lax.all_gather(current, "row", axis=1, tiled=True),
+            jnp.concatenate(
+                lax.all_to_all(jnp.stack([current] * lax.axis_size("row")), "row", 0, 0), axis=1
+            ),
             preferred_element_type=jnp.float32,
         )
         grouped = partial_value.reshape(local_rows, row_count, col_count, per_device)

time: 550 us -> 627 us (1.14)
  blocking collectives: 99 us -> 238 us
  waiting for transfers between devices: 198 us -> 70.3 us
  local copies, waits for them, and re-layouts: 150 us -> 215 us
    all_to_all x0 -> x2, blocking collectives: none -> 141 us  [body(): lax.all_to_all(jnp.stack([current] * lax.axis_size('row')), 'row', 0, 0)]
    all_gather x2 -> x0, waiting for transfers between devices: 127 us -> none  [body(): lax.all_gather(current, 'row', axis=1, tiled=True)]
    slice x174, local copies, waits for them, and re-layouts: 35.8 us -> 65.1 us  [spread_levels(): pieces.append(halves[:, start:start + count, :])]
    reshape x0 -> x2, local copies, waits for them, and re-layouts: none -> 14.7 us  [body(): jnp.concatenate(lax.all_to_all(jnp.stack([current] * lax.axis_size('row')...]
    unnamed x185 -> x191, local copies, waits for them, and re-layouts: 27.3 us -> 39.6 us
    dot_general x0 -> x1, local copies, waits for them, and re-layouts: none -> 8.14 us  [body(): jnp.dot(tmatrix, jnp.concatenate(lax.all_to_all(jnp.stack([current] * lax...]
  transfers between devices with their start and end apart: 5 -> 3, of which waited for: 5 -> 3; matrix products, arithmetic and copies ran while one was open for 0% -> 0% of each run, Pallas kernels for 0% -> 0%
where the time goes in v1:
time: 627 us; the launch traced here: 620 us
  blocking collectives  238 us (38%)
  local copies, waits for them, and re-layouts  215 us (34%)
  waiting for transfers between devices  70.3 us (11%)
  matrix products  66.3 us (11%)
  between operations  16 us (3%)
  starting transfers between devices  7.52 us (1%)
  other arithmetic  6.51 us (1%)
    all_to_all x2, blocking collectives, body(): lax.all_to_all(jnp.stack([current] * lax.axis_size('row')), 'row', 0, 0)  141 us
    all_to_all x2, blocking collectives, body(): lax.all_to_all(grouped.astype(jnp.bfloat16), 'row', split_axis=1, concat_...  82.5 us
    slice x174, local copies, waits for them, and re-layouts, spread_levels(): pieces.append(halves[:, start:start + count, :])  65.1 us
    reduce_scatter x2, waiting for transfers between devices, body(): lax.psum_scatter(regrouped.astype(jnp.float32).astype(jnp.bfloat16), 'col...  62.7 us
    unnamed x191, local copies, waits for them, and re-layouts  39.6 us
    squeeze x161, local copies, waits for them, and re-layouts, pick_levels(): pieces.append(projected[:, freq_index, skip:, :])  23 us
    all_to_all x4, local copies, waits for them, and re-layouts, body(): lax.all_to_all(grouped.astype(jnp.bfloat16), 'row', split_axis=1, concat_...  20.5 us
    dot_general x2, matrix products, contrast_apply(): jnp.einsum('qlt,cktq->cqlk', legendre_wide, spectrum, precision=triple, p...  19.7 us
  transfers between devices with their start and end apart: 3, of which 3 were waited for; matrix products, arithmetic and copies ran while one was open for 0% of the time, Pallas kernels for 0%

profile of v1, /device:TPU:1, one launch (start us, length us, event | category | flops | bytes accessed | tf_op | source)
XLA Modules:
  0.0 619.8 jit_solution(7573031915973509975)
XLA Ops:
  6.5 1.8 stack.8
  8.4 72.0 %all_to_all.64 = bf16[16,1332,128]{2,1,0:T(8,128)(2,1)S(1)} all-to-all(bf16[16,1332,128]{2,1,0:T(8,128)(2,1)S(1)} %stack.8), channel_id=1, replica_groups=mesh['row'=16,'col'=8] {'row'}, dimensions={0} | all-to-all | bytes 10911744 | tf_op jit(solution)/shard_map/all_to_all | solution.py:125
  80.4 7.4 %copy.175 = bf16[1332,16,128]{2,1,0:T(8,128)(2,1)S(1)} copy(bf16[1332,16,128]{2,0,1:T(8,128)(2,1)S(1)} %bitcast.680) | data formatting | bytes 10911744 | tf_op jit(solution)/shard_map/reshape | solution.py:124
  87.7 1.0 pad.8
  88.8 5.1 copy.243
  93.9 8.1 %copy.176 = bf16[2048,1332]{1,0:T(8,128)(2,1)} copy(bf16[2048,1332]{0,1:T(8,128)(2,1)} %bitcast.682) | data formatting | bytes 10911744 | tf_op jit(solution)/shard_map/dot_general | solution.py:122
  102.0 8.2 %convolution_convert_fusion.1 = bf16[666,16,8,16]{0,3,2,1:T(8,128)(2,1)S(1)} fusion(bf16[16,8,16,1332]{3,2,1,0:T(8,128)(2,1)} %bitcast.687, bf16[666,1332]{1,0:T(8,128)(2,1)S(1)} %copy-done), kind=kOutput, calls=%fused_computation.22 | convolution fusion | flops 3634974720 | bytes 9958032 | tf_op jit(solution)/shard_map/dot_general | solution.py:122
  110.2 40.4 %all_to_all.65 = bf16[666,16,8,16]{0,3,2,1:T(8,128)(2,1)S(1)} all-to-all(bf16[666,16,8,16]{0,3,2,1:T(8,128)(2,1)S(1)} %convolution_convert_fusion.1), channel_id=1, replica_groups=mesh['row'=16,'col'=8] {'row'}, dimensions={1} | all-to-all | bytes 5455872 | tf_op jit(solution)/shard_map/all_to_all | solution.py:130
  150.6 3.4 copy.177
  154.0 6.9 %all_to_all.50 = bf16[10656,1,8,16]{0,3,2,1:T(8,128)(2,1)} reshape(bf16[16,666,1,8,16]{1,0,4,3,2:T(8,128)(2,1)} %copy.177) | data formatting | bytes 5455872 | tf_op jit(solution)/shard_map/all_to_all | solution.py:130
  160.9 1.1 copy-done.11
  162.0 0.9 slice_bitcast_fusion.2
  162.9 31.9 %reduce-scatter.3.cloned.1.call-done = bf16[10656,1,1,16]{0,3,2,1:T(8,128)(2,1)} async-done(((bf16[10656,1,8,16]{0,3,2,1:T(8,128)(2,1)}), bf16[10656,1,1,16]{0,3,2,1:T(8,128)(2,1)}) %reduce-scatter.3.cloned.1.call-update) | async-done | bytes 341008 | tf_op jit(solution)/shard_map/reduce_scatter | solution.py:133
  194.7 1.3 reshape_reshape.6
  202.8 0.7 fusion.106
  206.9 0.7 fusion.112
  212.5 0.7 fusion.120
  218.7 0.7 fusion.129
  230.7 1.6 concatenate.24
  233.5 11.8 %concatenate.23 = bf16[2,9417,16]{1,0,2:T(2,128)(2,1)S(1)} concatenate(bf16[2,144,16]{1,0,2:T(2,128)(2,1)S(1)} %slice.2639, bf16[2,1,16]{1,0,2:T(2,128)(2,1)S(1)} %broadcast.227, bf16[2,71,16]{1,0,2:T(2,128)(2,1)} %get-tuple-element.457, bf16[2,2,16]{1,0,2:T(2,128)(2,1)S(1)} %broadcast.228, bf16[2,70,16]{1,0,2:T(2,128)(2,1)} %get-tuple-element.455, ...), dimensions={1} | concatenate | bytes 1205376
  245.7 1.5 pad_maximum_fusion
  247.2 3.9 reshape.80
  251.2 3.6 convolution_bitcast_fusion.1
  254.8 7.1 %fusion.8 = f32[2,16,144,288]{3,2,1,0:T(8,128)S(1)} fusion(f32[145,288,1,1]{1,0,3,2:T(8,128)S(1)} %copy-done.1, f32[2,16,144,145]{2,1,0,3:T(8,128)S(1)} %convolution_bitcast_fusion.1), kind=kOutput, calls=%fused_computation.10 | convolution fusion | flops 1154580480 | bytes 8148096 | tf_op jit(solution)/shard_map/cktq,qp->cktp/dot_general | solution.py:95
  261.9 0.7 multiply_add_fusion.3
  262.7 5.6 fusion
  268.3 6.5 %copy.181 = f32[2,16,144,145]{2,1,0,3:T(8,128)} copy(f32[2,16,144,145]{3,2,1,0:T(8,128)} %fusion) | data formatting | bytes 5345280 | tf_op jit(solution)/shard_map/cktp,qp->cktq/dot_general | solution.py:101
  274.8 9.8 %fusion.14 = bf16[2,145,72,16]{2,3,0,1:T(8,128)(2,1)S(1)} fusion(f32[2,16,144,145]{2,1,0,3:T(8,128)} %copy.181, f32[145,72,144,1]{2,1,3,0:T(8,128)} %constant.13), kind=kOutput, calls=%fused_computation.26 | convolution fusion | flops 288979200 | bytes 9354240 | tf_op jit(solution)/shard_map/qlt,cktq->cqlk/dot_general | solution.py:104
  301.0 1.5 concatenate.17
  303.1 0.8 copy.197
  303.9 7.5 %all-to-all-start.2 = ((bf16[8,1332,1,16]{1,3,2,0:T(8,128)(2,1)}), bf16[8,1332,1,16]{1,3,2,0:T(8,128)(2,1)}, u32[]{:S(2)}, u32[]{:S(2)}) async-start(bf16[8,1332,1,16]{1,3,2,0:T(8,128)(2,1)} %copy.197), calls=%async_computation.3 | async-start | bytes 720896 | tf_op jit(solution)/shard_map/all_to_all | solution.py:141
  311.7 7.6 %all-to-all-done.2 = bf16[8,1332,1,16]{1,3,2,0:T(8,128)(2,1)} async-done(((bf16[8,1332,1,16]{1,3,2,0:T(8,128)(2,1)}), bf16[8,1332,1,16]{1,3,2,0:T(8,128)(2,1)}, u32[]{:S(2)}, u32[]{:S(2)}) %all-to-all-start.2) | async-done | bytes 341024 | tf_op jit(solution)/shard_map/all_to_all | solution.py:141
  319.3 1.0 bitcast_convert_fusion.1
  320.3 0.8 fusion.18
  321.1 1.2 copy.198
  322.3 0.7 stack.10
  323.1 69.2 %all_to_all.66 = bf16[16,1332,128]{2,1,0:T(8,128)(2,1)S(1)} all-to-all(bf16[16,1332,128]{2,1,0:T(8,128)(2,1)S(1)} %stack.10), channel_id=1, replica_groups=mesh['row'=16,'col'=8] {'row'}, dimensions={0} | all-to-all | bytes 10911744 | tf_op jit(solution)/shard_map/all_to_all | solution.py:125
  392.3 7.4 %copy.199 = bf16[1332,16,128]{2,1,0:T(8,128)(2,1)S(1)} copy(bf16[1332,16,128]{2,0,1:T(8,128)(2,1)S(1)} %bitcast.683) | data formatting | bytes 10911744 | tf_op jit(solution)/shard_map/reshape | solution.py:124
  399.7 1.0 pad.9
  400.7 2.8 copy.244
  403.5 5.9 fusion.12
  409.3 4.7 copy.200
  414.0 42.0 %all_to_all.67 = bf16[666,16,8,16]{0,3,2,1:T(8,128)(2,1)S(1)} all-to-all(bf16[666,16,8,16]{0,3,2,1:T(8,128)(2,1)} %bitcast.685), channel_id=1, replica_groups=mesh['row'=16,'col'=8] {'row'}, dimensions={1} | all-to-all | bytes 5455872 | tf_op jit(solution)/shard_map/all_to_all | solution.py:130
  456.1 3.4 copy.201
  459.5 6.9 %all_to_all.56 = bf16[10656,1,8,16]{0,3,2,1:T(8,128)(2,1)} reshape(bf16[16,666,1,8,16]{1,0,4,3,2:T(8,128)(2,1)} %copy.201) | data formatting | bytes 5455872 | tf_op jit(solution)/shard_map/all_to_all | solution.py:130
  466.4 30.8 %reduce-scatter.5.cloned.1.call-done = bf16[10656,1,1,16]{0,3,2,1:T(8,128)(2,1)} async-done(((bf16[10656,1,8,16]{0,3,2,1:T(8,128)(2,1)}), bf16[10656,1,1,16]{0,3,2,1:T(8,128)(2,1)}) %reduce-scatter.5.cloned.1.call-update) | async-done | bytes 341008 | tf_op jit(solution)/shard_map/reduce_scatter | solution.py:133
  497.1 1.3 reshape_reshape.7
  508.4 0.7 fusion.42
  518.0 0.7 fusion.56
  523.6 0.7 fusion.64
  529.8 0.7 fusion.73
  535.7 1.6 concatenate.21
  537.7 13.0 %concatenate.20 = bf16[2,9417,16]{1,0,2:T(2,128)(2,1)S(1)} concatenate(bf16[2,144,16]{1,0,2:T(2,128)(2,1)S(1)} %slice.2929, bf16[2,1,16]{1,0,2:T(2,128)(2,1)S(1)} %broadcast.227, bf16[2,71,16]{1,0,2:T(2,128)(2,1)} %get-tuple-element.345, bf16[2,2,16]{1,0,2:T(2,128)(2,1)S(1)} %broadcast.228, bf16[2,70,16]{1,0,2:T(2,128)(2,1)} %get-tuple-element.343, ...), dimensions={1} | concatenate | bytes 1205376
  550.7 1.5 pad_maximum_fusion.1
  552.2 3.7 reshape.81
  555.9 3.5 convolution_bitcast_fusion
  559.4 7.1 %fusion.6 = f32[2,16,144,288]{3,2,1,0:T(8,128)S(1)} fusion(f32[145,288,1,1]{1,0,3,2:T(8,128)S(1)} %copy-done.1, f32[2,16,144,145]{2,1,0,3:T(8,128)S(1)} %convolution_bitcast_fusion), kind=kOutput, calls=%fused_computation.8 | convolution fusion | flops 1154580480 | bytes 8148096 | tf_op jit(solution)/shard_map/cktq,qp->cktp/dot_general | solution.py:95
  566.6 0.7 multiply_add_fusion.1
  567.3 5.6 fusion.3
  573.0 6.5 %copy.205 = f32[2,16,144,145]{2,1,0,3:T(8,128)} copy(f32[2,16,144,145]{3,2,1,0:T(8,128)} %fusion.3) | data formatting | bytes 5345280 | tf_op jit(solution)/shard_map/cktp,qp->cktq/dot_general | solution.py:101
  579.5 9.8 %fusion.15 = bf16[2,145,72,16]{2,3,0,1:T(8,128)(2,1)S(1)} fusion(f32[2,16,144,145]{2,1,0,3:T(8,128)} %copy.205, f32[145,72,144,1]{2,1,3,0:T(8,128)} %constant.13), kind=kOutput, calls=%fused_computation.27 | convolution fusion | flops 288979200 | bytes 9354240 | tf_op jit(solution)/shard_map/qlt,cktq->cqlk/dot_general | solution.py:104
  596.1 0.9 concatenate.19
  597.6 14.0 %all_to_all.68 = bf16[8,1332,1,16]{1,3,2,0:T(8,128)(2,1)S(1)} all-to-all(bf16[8,1332,1,16]{1,3,2,0:T(8,128)(2,1)S(1)} %copy.221), channel_id=1, replica_groups=mesh['row'=16,'col'=8] {'col'}, dimensions={0} | all-to-all | bytes 681984 | tf_op jit(solution)/shard_map/all_to_all | solution.py:141
  611.8 0.9 copy.222
  (591 shorter events, 91.0 us)
Async XLA Ops:
  6.5 95.5 %copy-start = (bf16[666,1332]{1,0:T(8,128)(2,1)S(1)}, bf16[666,1332]{1,0:T(8,128)(2,1)}, u32[]{:S(2)}) copy-start(bf16[666,1332]{1,0:T(8,128)(2,1)} %param.11) | copy-start | bytes 5322676
  6.5 188.2 %reduce-scatter.3.cloned.1.call-start = ((), (), s32[]{:S(2)}) async-start(), calls=%async_computation.8 | async-start | bytes 3096576 | tf_op jit(solution)/shard_map/reduce_scatter | solution.py:133
  224.6 20.7 %copy-start.82 = (bf16[2,58,16]{1,0,2:T(2,128)(2,1)}, bf16[2,58,16]{1,0,2:T(2,128)(2,1)S(1)}, u32[]{:S(2)}) copy-start(bf16[2,58,16]{1,0,2:T(2,128)(2,1)S(1)} %broadcast.284) | copy-start | bytes 11140
  224.6 20.7 %copy-start.84 = (bf16[2,59,16]{1,0,2:T(2,128)(2,1)}, bf16[2,59,16]{1,0,2:T(2,128)(2,1)S(1)}, u32[]{:S(2)}) copy-start(bf16[2,59,16]{1,0,2:T(2,128)(2,1)S(1)} %broadcast.285) | copy-start | bytes 11332
  224.6 20.7 %copy-start.86 = (bf16[2,60,16]{1,0,2:T(2,128)(2,1)}, bf16[2,60,16]{1,0,2:T(2,128)(2,1)S(1)}, u32[]{:S(2)}) copy-start(bf16[2,60,16]{1,0,2:T(2,128)(2,1)S(1)} %broadcast.286) | copy-start | bytes 11524
  224.7 20.7 %copy-start.88 = (bf16[2,61,16]{1,0,2:T(2,128)(2,1)}, bf16[2,61,16]{1,0,2:T(2,128)(2,1)S(1)}, u32[]{:S(2)}) copy-start(bf16[2,61,16]{1,0,2:T(2,128)(2,1)S(1)} %broadcast.287) | copy-start | bytes 11716
  232.6 12.7 %copy-start.12 = (bf16[2,23,16]{1,0,2:T(2,128)(2,1)}, bf16[2,23,16]{1,0,2:T(2,128)(2,1)S(1)}, u32[]{:S(2)}) copy-start(bf16[2,23,16]{1,0,2:T(2,128)(2,1)S(1)} %broadcast.249) | copy-start | bytes 4420
  232.7 12.7 %copy-start.14 = (bf16[2,24,16]{1,0,2:T(2,128)(2,1)}, bf16[2,24,16]{1,0,2:T(2,128)(2,1)S(1)}, u32[]{:S(2)}) copy-start(bf16[2,24,16]{1,0,2:T(2,128)(2,1)S(1)} %broadcast.250) | copy-start | bytes 4612
  232.7 12.7 %copy-start.16 = (bf16[2,25,16]{1,0,2:T(2,128)(2,1)}, bf16[2,25,16]{1,0,2:T(2,128)(2,1)S(1)}, u32[]{:S(2)}) copy-start(bf16[2,25,16]{1,0,2:T(2,128)(2,1)S(1)} %broadcast.251) | copy-start | bytes 4804
  232.7 12.7 %copy-start.18 = (bf16[2,26,16]{1,0,2:T(2,128)(2,1)}, bf16[2,26,16]{1,0,2:T(2,128)(2,1)S(1)}, u32[]{:S(2)}) copy-start(bf16[2,26,16]{1,0,2:T(2,128)(2,1)S(1)} %broadcast.252) | copy-start | bytes 4996
  232.7 12.7 %copy-start.20 = (bf16[2,27,16]{1,0,2:T(2,128)(2,1)}, bf16[2,27,16]{1,0,2:T(2,128)(2,1)S(1)}, u32[]{:S(2)}) copy-start(bf16[2,27,16]{1,0,2:T(2,128)(2,1)S(1)} %broadcast.253) | copy-start | bytes 5188
  232.8 12.7 %copy-start.22 = (bf16[2,28,16]{1,0,2:T(2,128)(2,1)}, bf16[2,28,16]{1,0,2:T(2,128)(2,1)S(1)}, u32[]{:S(2)}) copy-start(bf16[2,28,16]{1,0,2:T(2,128)(2,1)S(1)} %broadcast.254) | copy-start | bytes 5380
  232.8 12.6 %copy-start.24 = (bf16[2,29,16]{1,0,2:T(2,128)(2,1)}, bf16[2,29,16]{1,0,2:T(2,128)(2,1)S(1)}, u32[]{:S(2)}) copy-start(bf16[2,29,16]{1,0,2:T(2,128)(2,1)S(1)} %broadcast.255) | copy-start | bytes 5572
  232.8 12.6 %copy-start.26 = (bf16[2,30,16]{1,0,2:T(2,128)(2,1)}, bf16[2,30,16]{1,0,2:T(2,128)(2,1)S(1)}, u32[]{:S(2)}) copy-start(bf16[2,30,16]{1,0,2:T(2,128)(2,1)S(1)} %broadcast.256) | copy-start | bytes 5764
  232.8 12.6 %copy-start.28 = (bf16[2,31,16]{1,0,2:T(2,128)(2,1)}, bf16[2,31,16]{1,0,2:T(2,128)(2,1)S(1)}, u32[]{:S(2)}) copy-start(bf16[2,31,16]{1,0,2:T(2,128)(2,1)S(1)} %broadcast.257) | copy-start | bytes 5956
  232.9 12.6 %copy-start.30 = (bf16[2,32,16]{1,0,2:T(2,128)(2,1)}, bf16[2,32,16]{1,0,2:T(2,128)(2,1)S(1)}, u32[]{:S(2)}) copy-start(bf16[2,32,16]{1,0,2:T(2,128)(2,1)S(1)} %broadcast.258) | copy-start | bytes 6148
  232.9 12.6 %copy-start.32 = (bf16[2,33,16]{1,0,2:T(2,128)(2,1)}, bf16[2,33,16]{1,0,2:T(2,128)(2,1)S(1)}, u32[]{:S(2)}) copy-start(bf16[2,33,16]{1,0,2:T(2,128)(2,1)S(1)} %broadcast.259) | copy-start | bytes 6340
  232.9 12.6 %copy-start.34 = (bf16[2,34,16]{1,0,2:T(2,128)(2,1)}, bf16[2,34,16]{1,0,2:T(2,128)(2,1)S(1)}, u32[]{:S(2)}) copy-start(bf16[2,34,16]{1,0,2:T(2,128)(2,1)S(1)} %broadcast.260) | copy-start | bytes 6532
  232.9 12.6 %copy-start.36 = (bf16[2,35,16]{1,0,2:T(2,128)(2,1)}, bf16[2,35,16]{1,0,2:T(2,128)(2,1)S(1)}, u32[]{:S(2)}) copy-start(bf16[2,35,16]{1,0,2:T(2,128)(2,1)S(1)} %broadcast.261) | copy-start | bytes 6724
  233.0 12.5 %copy-start.38 = (bf16[2,36,16]{1,0,2:T(2,128)(2,1)}, bf16[2,36,16]{1,0,2:T(2,128)(2,1)S(1)}, u32[]{:S(2)}) copy-start(bf16[2,36,16]{1,0,2:T(2,128)(2,1)S(1)} %broadcast.262) | copy-start | bytes 6916
  233.0 12.5 %copy-start.40 = (bf16[2,37,16]{1,0,2:T(2,128)(2,1)}, bf16[2,37,16]{1,0,2:T(2,128)(2,1)S(1)}, u32[]{:S(2)}) copy-start(bf16[2,37,16]{1,0,2:T(2,128)(2,1)S(1)} %broadcast.263) | copy-start | bytes 7108
  233.0 12.5 %copy-start.42 = (bf16[2,38,16]{1,0,2:T(2,128)(2,1)}, bf16[2,38,16]{1,0,2:T(2,128)(2,1)S(1)}, u32[]{:S(2)}) copy-start(bf16[2,38,16]{1,0,2:T(2,128)(2,1)S(1)} %broadcast.264) | copy-start | bytes 7300
  303.9 15.4 %all-to-all-start.2 = ((bf16[8,1332,1,16]{1,3,2,0:T(8,128)(2,1)}), bf16[8,1332,1,16]{1,3,2,0:T(8,128)(2,1)}, u32[]{:S(2)}, u32[]{:S(2)}) async-start(bf16[8,1332,1,16]{1,3,2,0:T(8,128)(2,1)} %copy.197), calls=%async_computation.3 | async-start | bytes 720896 | tf_op jit(solution)/shard_map/all_to_all | solution.py:141
  311.4 185.7 %reduce-scatter.5.cloned.1.call-start = ((), (), s32[]{:S(2)}) async-start(), calls=%async_computation.9 | async-start | bytes 3096576 | tf_op jit(solution)/shard_map/reduce_scatter | solution.py:133
  498.5 37.2 %copy-start.83 = (bf16[2,58,16]{1,0,2:T(2,128)(2,1)S(1)}, bf16[2,58,16]{1,0,2:T(2,128)(2,1)}, u32[]{:S(2)}) copy-start(bf16[2,58,16]{1,0,2:T(2,128)(2,1)} %copy-done.82) | copy-start | bytes 11140
  498.5 37.2 %copy-start.85 = (bf16[2,59,16]{1,0,2:T(2,128)(2,1)S(1)}, bf16[2,59,16]{1,0,2:T(2,128)(2,1)}, u32[]{:S(2)}) copy-start(bf16[2,59,16]{1,0,2:T(2,128)(2,1)} %copy-done.84) | copy-start | bytes 11332
  498.5 37.2 %copy-start.87 = (bf16[2,60,16]{1,0,2:T(2,128)(2,1)S(1)}, bf16[2,60,16]{1,0,2:T(2,128)(2,1)}, u32[]{:S(2)}) copy-start(bf16[2,60,16]{1,0,2:T(2,128)(2,1)} %copy-done.86) | copy-start | bytes 11524
  498.5 37.2 %copy-start.89 = (bf16[2,61,16]{1,0,2:T(2,128)(2,1)S(1)}, bf16[2,61,16]{1,0,2:T(2,128)(2,1)}, u32[]{:S(2)}) copy-start(bf16[2,61,16]{1,0,2:T(2,128)(2,1)} %copy-done.88) | copy-start | bytes 11716
  504.6 32.7 %copy-start.13 = (bf16[2,23,16]{1,0,2:T(2,128)(2,1)S(1)}, bf16[2,23,16]{1,0,2:T(2,128)(2,1)}, u32[]{:S(2)}) copy-start(bf16[2,23,16]{1,0,2:T(2,128)(2,1)} %copy-done.12) | copy-start | bytes 4420
  504.6 32.7 %copy-start.15 = (bf16[2,24,16]{1,0,2:T(2,128)(2,1)S(1)}, bf16[2,24,16]{1,0,2:T(2,128)(2,1)}, u32[]{:S(2)}) copy-start(bf16[2,24,16]{1,0,2:T(2,128)(2,1)} %copy-done.14) | copy-start | bytes 4612
  504.6 32.7 %copy-start.17 = (bf16[2,25,16]{1,0,2:T(2,128)(2,1)S(1)}, bf16[2,25,16]{1,0,2:T(2,128)(2,1)}, u32[]{:S(2)}) copy-start(bf16[2,25,16]{1,0,2:T(2,128)(2,1)} %copy-done.16) | copy-start | bytes 4804
  504.7 32.7 %copy-start.19 = (bf16[2,26,16]{1,0,2:T(2,128)(2,1)S(1)}, bf16[2,26,16]{1,0,2:T(2,128)(2,1)}, u32[]{:S(2)}) copy-start(bf16[2,26,16]{1,0,2:T(2,128)(2,1)} %copy-done.18) | copy-start | bytes 4996
  504.7 32.7 %copy-start.21 = (bf16[2,27,16]{1,0,2:T(2,128)(2,1)S(1)}, bf16[2,27,16]{1,0,2:T(2,128)(2,1)}, u32[]{:S(2)}) copy-start(bf16[2,27,16]{1,0,2:T(2,128)(2,1)} %copy-done.20) | copy-start | bytes 5188
  504.7 32.7 %copy-start.23 = (bf16[2,28,16]{1,0,2:T(2,128)(2,1)S(1)}, bf16[2,28,16]{1,0,2:T(2,128)(2,1)}, u32[]{:S(2)}) copy-start(bf16[2,28,16]{1,0,2:T(2,128)(2,1)} %copy-done.22) | copy-start | bytes 5380
  504.7 32.7 %copy-start.25 = (bf16[2,29,16]{1,0,2:T(2,128)(2,1)S(1)}, bf16[2,29,16]{1,0,2:T(2,128)(2,1)}, u32[]{:S(2)}) copy-start(bf16[2,29,16]{1,0,2:T(2,128)(2,1)} %copy-done.24) | copy-start | bytes 5572
  504.7 32.7 %copy-start.27 = (bf16[2,30,16]{1,0,2:T(2,128)(2,1)S(1)}, bf16[2,30,16]{1,0,2:T(2,128)(2,1)}, u32[]{:S(2)}) copy-start(bf16[2,30,16]{1,0,2:T(2,128)(2,1)} %copy-done.26) | copy-start | bytes 5764
  504.7 32.7 %copy-start.29 = (bf16[2,31,16]{1,0,2:T(2,128)(2,1)S(1)}, bf16[2,31,16]{1,0,2:T(2,128)(2,1)}, u32[]{:S(2)}) copy-start(bf16[2,31,16]{1,0,2:T(2,128)(2,1)} %copy-done.28) | copy-start | bytes 5956
  504.7 32.7 %copy-start.31 = (bf16[2,32,16]{1,0,2:T(2,128)(2,1)S(1)}, bf16[2,32,16]{1,0,2:T(2,128)(2,1)}, u32[]{:S(2)}) copy-start(bf16[2,32,16]{1,0,2:T(2,128)(2,1)} %copy-done.30) | copy-start | bytes 6148
  504.7 32.7 %copy-start.33 = (bf16[2,33,16]{1,0,2:T(2,128)(2,1)S(1)}, bf16[2,33,16]{1,0,2:T(2,128)(2,1)}, u32[]{:S(2)}) copy-start(bf16[2,33,16]{1,0,2:T(2,128)(2,1)} %copy-done.32) | copy-start | bytes 6340
  504.7 32.7 %copy-start.35 = (bf16[2,34,16]{1,0,2:T(2,128)(2,1)S(1)}, bf16[2,34,16]{1,0,2:T(2,128)(2,1)}, u32[]{:S(2)}) copy-start(bf16[2,34,16]{1,0,2:T(2,128)(2,1)} %copy-done.34) | copy-start | bytes 6532
  504.7 32.7 %copy-start.37 = (bf16[2,35,16]{1,0,2:T(2,128)(2,1)S(1)}, bf16[2,35,16]{1,0,2:T(2,128)(2,1)}, u32[]{:S(2)}) copy-start(bf16[2,35,16]{1,0,2:T(2,128)(2,1)} %copy-done.36) | copy-start | bytes 6724
  504.7 32.7 %copy-start.39 = (bf16[2,36,16]{1,0,2:T(2,128)(2,1)S(1)}, bf16[2,36,16]{1,0,2:T(2,128)(2,1)}, u32[]{:S(2)}) copy-start(bf16[2,36,16]{1,0,2:T(2,128)(2,1)} %copy-done.38) | copy-start | bytes 6916
  504.8 32.7 %copy-start.41 = (bf16[2,37,16]{1,0,2:T(2,128)(2,1)S(1)}, bf16[2,37,16]{1,0,2:T(2,128)(2,1)}, u32[]{:S(2)}) copy-start(bf16[2,37,16]{1,0,2:T(2,128)(2,1)} %copy-done.40) | copy-start | bytes 7108
  504.8 32.7 %copy-start.43 = (bf16[2,38,16]{1,0,2:T(2,128)(2,1)S(1)}, bf16[2,38,16]{1,0,2:T(2,128)(2,1)}, u32[]{:S(2)}) copy-start(bf16[2,38,16]{1,0,2:T(2,128)(2,1)} %copy-done.42) | copy-start | bytes 7300
  504.8 32.7 %copy-start.45 = (bf16[2,39,16]{1,0,2:T(2,128)(2,1)S(1)}, bf16[2,39,16]{1,0,2:T(2,128)(2,1)}, u32[]{:S(2)}) copy-start(bf16[2,39,16]{1,0,2:T(2,128)(2,1)} %copy-done.44) | copy-start | bytes 7492
  504.8 32.7 %copy-start.47 = (bf16[2,40,16]{1,0,2:T(2,128)(2,1)S(1)}, bf16[2,40,16]{1,0,2:T(2,128)(2,1)}, u32[]{:S(2)}) copy-start(bf16[2,40,16]{1,0,2:T(2,128)(2,1)} %copy-done.46) | copy-start | bytes 7684
  504.8 32.7 %copy-start.49 = (bf16[2,41,16]{1,0,2:T(2,128)(2,1)S(1)}, bf16[2,41,16]{1,0,2:T(2,128)(2,1)}, u32[]{:S(2)}) copy-start(bf16[2,41,16]{1,0,2:T(2,128)(2,1)} %copy-done.48) | copy-start | bytes 7876
  504.8 32.7 %copy-start.51 = (bf16[2,42,16]{1,0,2:T(2,128)(2,1)S(1)}, bf16[2,42,16]{1,0,2:T(2,128)(2,1)}, u32[]{:S(2)}) copy-start(bf16[2,42,16]{1,0,2:T(2,128)(2,1)} %copy-done.50) | copy-start | bytes 8068
  504.8 32.7 %copy-start.53 = (bf16[2,43,16]{1,0,2:T(2,128)(2,1)S(1)}, bf16[2,43,16]{1,0,2:T(2,128)(2,1)}, u32[]{:S(2)}) copy-start(bf16[2,43,16]{1,0,2:T(2,128)(2,1)} %copy-done.52) | copy-start | bytes 8260
  504.8 32.7 %copy-start.55 = (bf16[2,44,16]{1,0,2:T(2,128)(2,1)S(1)}, bf16[2,44,16]{1,0,2:T(2,128)(2,1)}, u32[]{:S(2)}) copy-start(bf16[2,44,16]{1,0,2:T(2,128)(2,1)} %copy-done.54) | copy-start | bytes 8452
  504.8 32.7 %copy-start.57 = (bf16[2,45,16]{1,0,2:T(2,128)(2,1)S(1)}, bf16[2,45,16]{1,0,2:T(2,128)(2,1)}, u32[]{:S(2)}) copy-start(bf16[2,45,16]{1,0,2:T(2,128)(2,1)} %copy-done.56) | copy-start | bytes 8644
  504.8 32.7 %copy-start.59 = (bf16[2,46,16]{1,0,2:T(2,128)(2,1)S(1)}, bf16[2,46,16]{1,0,2:T(2,128)(2,1)}, u32[]{:S(2)}) copy-start(bf16[2,46,16]{1,0,2:T(2,128)(2,1)} %copy-done.58) | copy-start | bytes 8836
  504.9 32.7 %copy-start.61 = (bf16[2,47,16]{1,0,2:T(2,128)(2,1)S(1)}, bf16[2,47,16]{1,0,2:T(2,128)(2,1)}, u32[]{:S(2)}) copy-start(bf16[2,47,16]{1,0,2:T(2,128)(2,1)} %copy-done.60) | copy-start | bytes 9028
  504.9 32.7 %copy-start.63 = (bf16[2,48,16]{1,0,2:T(2,128)(2,1)S(1)}, bf16[2,48,16]{1,0,2:T(2,128)(2,1)}, u32[]{:S(2)}) copy-start(bf16[2,48,16]{1,0,2:T(2,128)(2,1)} %copy-done.62) | copy-start | bytes 9220
  504.9 32.7 %copy-start.65 = (bf16[2,49,16]{1,0,2:T(2,128)(2,1)S(1)}, bf16[2,49,16]{1,0,2:T(2,128)(2,1)}, u32[]{:S(2)}) copy-start(bf16[2,49,16]{1,0,2:T(2,128)(2,1)} %copy-done.64) | copy-start | bytes 9412
  504.9 32.7 %copy-start.67 = (bf16[2,50,16]{1,0,2:T(2,128)(2,1)S(1)}, bf16[2,50,16]{1,0,2:T(2,128)(2,1)}, u32[]{:S(2)}) copy-start(bf16[2,50,16]{1,0,2:T(2,128)(2,1)} %copy-done.66) | copy-start | bytes 9604
  504.9 32.7 %copy-start.69 = (bf16[2,51,16]{1,0,2:T(2,128)(2,1)S(1)}, bf16[2,51,16]{1,0,2:T(2,128)(2,1)}, u32[]{:S(2)}) copy-start(bf16[2,51,16]{1,0,2:T(2,128)(2,1)} %copy-done.68) | copy-start | bytes 9796
  504.9 32.7 %copy-start.71 = (bf16[2,52,16]{1,0,2:T(2,128)(2,1)S(1)}, bf16[2,52,16]{1,0,2:T(2,128)(2,1)}, u32[]{:S(2)}) copy-start(bf16[2,52,16]{1,0,2:T(2,128)(2,1)} %copy-done.70) | copy-start | bytes 9988
  504.9 32.7 %copy-start.73 = (bf16[2,53,16]{1,0,2:T(2,128)(2,1)S(1)}, bf16[2,53,16]{1,0,2:T(2,128)(2,1)}, u32[]{:S(2)}) copy-start(bf16[2,53,16]{1,0,2:T(2,128)(2,1)} %copy-done.72) | copy-start | bytes 10180
  504.9 32.7 %copy-start.75 = (bf16[2,54,16]{1,0,2:T(2,128)(2,1)S(1)}, bf16[2,54,16]{1,0,2:T(2,128)(2,1)}, u32[]{:S(2)}) copy-start(bf16[2,54,16]{1,0,2:T(2,128)(2,1)} %copy-done.74) | copy-start | bytes 10372
  504.9 32.7 %copy-start.77 = (bf16[2,55,16]{1,0,2:T(2,128)(2,1)S(1)}, bf16[2,55,16]{1,0,2:T(2,128)(2,1)}, u32[]{:S(2)}) copy-start(bf16[2,55,16]{1,0,2:T(2,128)(2,1)} %copy-done.76) | copy-start | bytes 10564
  504.9 32.7 %copy-start.79 = (bf16[2,56,16]{1,0,2:T(2,128)(2,1)S(1)}, bf16[2,56,16]{1,0,2:T(2,128)(2,1)}, u32[]{:S(2)}) copy-start(bf16[2,56,16]{1,0,2:T(2,128)(2,1)} %copy-done.78) | copy-start | bytes 10756
  505.0 32.7 %copy-start.81 = (bf16[2,57,16]{1,0,2:T(2,128)(2,1)S(1)}, bf16[2,57,16]{1,0,2:T(2,128)(2,1)}, u32[]{:S(2)}) copy-start(bf16[2,57,16]{1,0,2:T(2,128)(2,1)} %copy-done.80) | copy-start | bytes 10948
  597.6 14.1 %copy-start.3 = (bf16[1332,128]{0,1:T(8,128)(2,1)S(1)}, bf16[1332,128]{0,1:T(8,128)(2,1)}, u32[]{:S(2)}) copy-start(bf16[1332,128]{0,1:T(8,128)(2,1)} %copy-done.2) | copy-start | bytes 1022980
  (30 other events, 301.4 us)
Sparse Core Ops, SparseCore 0:
  161.1 33.6 reduce-scatter.2
  466.5 30.6 reduce-scatter.4
